TPU v7x, 32 devices: a whole 2x2x4 slice. The times are simulated.
32 devices in a mesh: head: 2 (over y), seq: 16 (over z, x, core).
Axes of the slice: x: 2, y: 2, z: 4, core: 2. Of those that a mesh axis runs over, the one named last changes fastest.
Arguments:
- tokens: bfloat16 [12288, 2048], P('seq', 'head'), may hold values from -6 to 6
- weights: bfloat16 [3, 2048, 2048], P(None, 'seq', 'head'), may hold values from -0.06591797 to 0.06591797
- landmark_pos: int32 [16, 256], P('head'), may hold values from 0 to 12287, as said below
Outputs:
- attended: bfloat16 [12288, 2048], P('seq', 'head')
Inputs may be any that keep to these rules, and one draw needn't show every extreme that they name: `landmark_pos`: landmark number j of every head lies in tokens j * 48 to (j + 1) * 48 - 1.
All inputs are finite; a program needn't handle non-finite values. Where the computation divides by a largest or mean magnitude, that divisor is 1e-20 or more.
Results may differ from a plain program's by a relative error of at most 0.0041.
Values may be sent and summed in bfloat16 or wider, within the bound.
A program may use at most 64 MiB of HBM per device.

v0:
```python
import math

import jax
import jax.numpy as jnp
from jax import lax
from jax.sharding import PartitionSpec as P

NSTEPS = 6


def gauss(left, right):
    inner = jnp.einsum("hie,hje->hij", left, right, preferred_element_type=jnp.float32)
    left32 = left.astype(jnp.float32)
    right32 = right.astype(jnp.float32)
    dist = (
        jnp.sum(left32 * left32, -1)[:, :, None]
        + jnp.sum(right32 * right32, -1)[:, None, :]
        - 2.0 * inner
    )
    return jnp.exp(-dist / (2.0 * math.sqrt(left.shape[-1])))


def batched(left, right):
    return jnp.einsum("hij,hjk->hik", left, right, precision=lax.Precision.HIGHEST)


def gather_landmarks(query, keys, landmark_pos):
    per_group = landmark_pos.shape[1] // lax.axis_size("seq")
    tok_rows = query.shape[1]
    group = lax.axis_index("seq")
    local_pos = lax.dynamic_slice_in_dim(landmark_pos, group * per_group, per_group, 1)
    offsets = local_pos - group * tok_rows
    picker = (offsets[:, :, None] == jnp.arange(tok_rows, dtype=jnp.int32)[None, None, :]).astype(
        jnp.bfloat16
    )
    picked_q = jnp.einsum("hjt,hte->hje", picker, query, preferred_element_type=jnp.float32)
    picked_k = jnp.einsum("hjt,hte->hje", picker, keys, preferred_element_type=jnp.float32)
    number = group * per_group + jnp.arange(per_group, dtype=jnp.int32)
    even = (number % 2 == 0)[None, :, None]
    local_marks = jnp.where(even, picked_q, picked_k).astype(jnp.bfloat16)
    return lax.all_gather(local_marks, "seq", axis=1, tiled=True)


def shards(tokens, weights, landmark_pos):
    tok_rows = tokens.shape[0]
    heads_dev = landmark_pos.shape[0]
    head_cols = weights.shape[2]
    head_size = head_cols // heads_dev
    whole = lax.all_gather(tokens, "head", axis=1, tiled=True)

    def heads_of(flat):
        return jnp.transpose(
            flat.astype(jnp.bfloat16).reshape(tok_rows, heads_dev, head_size), (1, 0, 2)
        )

    projected = jnp.einsum(
        "td,kdc->ktc",
        whole,
        lax.all_gather(weights, "seq", axis=1, tiled=True),
        preferred_element_type=jnp.float32,
    )
    query = heads_of(projected[0])
    keys = heads_of(projected[1])
    values = heads_of(projected[2])
    landmarks = gather_landmarks(query, keys, landmark_pos)
    key_weights = gauss(landmarks, keys).astype(jnp.bfloat16)
    partial_sum = jnp.einsum(
        "hjt,hte->hje", key_weights, values, preferred_element_type=jnp.float32
    )
    summary = lax.psum(partial_sum, "seq")
    inner = gauss(landmarks, landmarks)
    scale_cols = jnp.max(jnp.sum(jnp.abs(inner), 1), axis=-1)
    scale_rows = jnp.max(jnp.sum(jnp.abs(inner), 2), axis=-1)
    iterate = inner / (scale_cols * scale_rows)[:, None, None]
    for step in range(NSTEPS):
        iterate = 2.0 * iterate - batched(batched(iterate, inner), iterate)
    mixed = batched(iterate, summary).astype(jnp.bfloat16)
    query_weights = gauss(query, landmarks).astype(jnp.bfloat16)
    result = jnp.einsum("htm,hme->the", query_weights, mixed, preferred_element_type=jnp.float32)
    return result.reshape(tok_rows, head_cols).astype(jnp.bfloat16)


def solution(mesh):
    return jax.shard_map(
        shards,
        mesh=mesh,
        in_specs=(P("seq", "head"), P(None, "seq", "head"), P("head", None)),
        out_specs=P("seq", "head"),
        check_vma=False,
    )
```

profile of v0, /device:TPU:0, one launch (start us, length us, event | category | flops | bytes accessed | tf_op | source)
XLA Modules:
  0.0 318.9 jit_solution(760819173314215912)
XLA Ops:
  9.0 47.6 %all-gather.5.cloned.1.call-done = bf16[768,2048]{1,0:T(8,128)(2,1)} async-done(((bf16[768,1024]{1,0:T(8,128)(2,1)}), bf16[768,2048]{1,0:T(8,128)(2,1)}) %all-gather.5.cloned.1.call-update) | async-done | bytes 3145744 | tf_op jit(solution)/shard_map/all_gather | solution.py:49
  56.6 106.1 %all-gather.3.cloned.1.call-done = bf16[3,2048,1024]{1,2,0:T(8,128)(2,1)} async-done(((bf16[3,128,1024]{1,2,0:T(8,128)(2,1)}), bf16[3,2048,1024]{1,2,0:T(8,128)(2,1)}) %all-gather.3.cloned.1.call-update) | async-done | bytes 12582928 | tf_op jit(solution)/shard_map/all_gather | solution.py:59
  162.7 14.0 %convert_bitcast_fusion = bf16[3,768,1024]{1,2,0:T(8,128)(2,1)S(1)} fusion(bf16[3,2048,1024]{1,2,0:T(8,128)(2,1)} %all-gather.3.cloned.1.call-done, bf16[768,2048]{1,0:T(8,128)(2,1)} %all-gather.5.cloned.1.call-done), kind=kOutput, calls=%fused_computation.2 | convolution fusion | flops 9666035712 | bytes 20447232 | tf_op jit(solution)/shard_map/td,kdc->ktc/dot_general | solution.py:56
  176.7 2.0 fusion.47
  178.7 1.9 copy.10
  183.2 20.6 %all_gather.11 = bf16[8,256,128]{2,1,0:T(8,128)(2,1)S(1)} all-gather(bf16[8,16,128]{2,1,0:T(8,128)(2,1)S(1)} %fusion.31), channel_id=1, replica_groups=mesh['head'=2,'seq'=16] {'seq'}, dimensions={1}, use_global_device_ids=true | all-gather | bytes 557056 | tf_op jit(solution)/shard_map/all_gather | solution.py:41
  204.1 1.3 fusion.46
  205.4 5.3 %fusion.3 = f32[8,256,128]{2,1,0:T(8,128)} fusion(bf16[8,768,128]{1,2,0:T(8,128)(2,1)} %bitcast.65, f32[8,768]{1,0:T(8,128)S(1)} %multiply_reduce_fusion.1, f32[8,256]{1,0:T(8,128)S(1)} %multiply_reduce_fusion.2, bf16[8,256,128]{2,1,0:T(8,128)(2,1)} %copy-done.5, bf16[768,8,128]{2,0,1:T(8,128)(2,1)} %copy-done.4), kind=kOutput, calls=%fused_computation.8 | convolution fusion | flops 814743552 | bytes 4751360 | tf_op jit(solution)/shard_map/hjt,hte->hje/dot_general | solution.py:67
  211.0 2.2 fusion.14
  213.2 2.5 multiply_subtract_fusion.4
  215.7 2.2 fusion.48
  217.9 2.3 multiply_subtract_fusion.3
  220.2 2.4 fusion.49
  222.6 2.3 multiply_subtract_fusion.2
  225.0 2.2 fusion.50
  227.1 2.3 multiply_subtract_fusion.1
  229.5 2.2 fusion.51
  231.7 2.6 multiply_subtract_fusion
  234.3 2.2 fusion.52
  237.4 3.5 %fusion.53 = f32[8,256,256]{2,1,0:T(8,128)} fusion(f32[8,256,256]{2,1,0:T(8,128)S(1)} %fusion.52, f32[8,256,256]{2,1,0:T(8,128)S(1)} %multiply_subtract_fusion), kind=kOutput, calls=%fused_computation.58 | convolution fusion | flops 1610612736 | bytes 6291456 | tf_op jit(solution)/shard_map/hij,hjk->hik/dot_general | solution.py:24
  240.9 59.8 %all-reduce.2.cloned.1.call-done = f32[8,256,128]{2,1,0:T(8,128)} async-done(((f32[8,256,128]{2,1,0:T(8,128)}), f32[8,256,128]{2,1,0:T(8,128)}) %all-reduce.2.cloned.1.call-update) | async-done | bytes 1048592 | tf_op jit(solution)/shard_map/psum | solution.py:70
  300.7 4.9 %fusion.25 = bf16[8,256,128]{1,2,0:T(8,128)(2,1)S(1)} fusion(f32[8,256,128]{2,1,0:T(8,128)} %all-reduce.2.cloned.1.call-done, f32[8,256,256]{2,1,0:T(8,128)} %fusion.53, f32[8,256,256]{2,1,0:T(8,128)} %copy-done), kind=kOutput, calls=%fused_computation.30 | convolution fusion | flops 806617088 | bytes 5767168 | tf_op jit(solution)/shard_map/hij,hjk->hik/dot_general | solution.py:24
  305.7 3.7 %fusion.13 = bf16[8,128,768]{2,1,0:T(8,128)(2,1)} fusion(bf16[8,256,128]{1,2,0:T(8,128)(2,1)S(1)} %fusion.25, f32[8,256]{1,0:T(8,128)S(1)} %multiply_reduce_fusion.2, f32[8,768]{1,0:T(8,128)S(1)} %multiply_reduce_fusion, bf16[8,256,128]{2,1,0:T(8,128)(2,1)S(1)} %copy-done.6, bf16[768,8,128]{2,0,1:T(8,128)(2,1)S(1)} %copy-done.3), kind=kOutput, calls=%fused_computation.20 | convolution fusion | flops 815529984 | bytes 4227072 | tf_op jit(solution)/shard_map/htm,hme->the/dot_general | solution.py:79
  309.4 2.6 copy.11
  (36 shorter events, 6.5 us)
Async XLA Ops:
  6.5 1.1 copy-start.7
  6.5 2.4 copy-start.8
  6.5 50.0 %all-gather.5.cloned.1.call-start = ((), (), s32[]{:S(2)}) async-start(), calls=%async_computation.1 | async-start | bytes 4718592 | tf_op jit(solution)/shard_map/all_gather | solution.py:49
  7.3 155.4 %all-gather.3.cloned.1.call-start = ((), (), s32[]{:S(2)}) async-start(), calls=%async_computation | async-start | bytes 13369344 | tf_op jit(solution)/shard_map/all_gather | solution.py:59
  8.8 291.9 %all-reduce.2.cloned.1.call-start = ((), (), s32[]{:S(2)}) async-start(), calls=%async_computation.2 | async-start | bytes 2097152 | tf_op jit(solution)/shard_map/psum | solution.py:70
  180.6 1.3 copy-start.4
  182.8 21.0 %copy-start.1 = (bf16[768,8,128]{2,0,1:T(8,128)(2,1)}, bf16[768,8,128]{2,0,1:T(8,128)(2,1)S(1)}, u32[]{:S(2)}) copy-start(bf16[768,8,128]{2,0,1:T(8,128)(2,1)S(1)} %copy.9) | copy-start | bytes 4718596
  203.8 1.7 copy-start.5
  234.2 3.1 copy-start
  234.3 2.2 copy-start.2
  240.9 64.8 %copy-start.3 = (bf16[768,8,128]{2,0,1:T(8,128)(2,1)S(1)}, bf16[768,8,128]{2,0,1:T(8,128)(2,1)}, u32[]{:S(2)}) copy-start(bf16[768,8,128]{2,0,1:T(8,128)(2,1)} %copy-done.1) | copy-start | bytes 4718596
  240.9 64.8 %copy-start.6 = (bf16[8,256,128]{2,1,0:T(8,128)(2,1)S(1)}, bf16[8,256,128]{2,1,0:T(8,128)(2,1)}, u32[]{:S(2)}) copy-start(bf16[8,256,128]{2,1,0:T(8,128)(2,1)} %copy-done.5) | copy-start | bytes 1572868
Sparse Core Ops, SparseCore 0:
  8.9 47.6 all-gather.4
  58.7 103.9 all-gather.2
  210.8 89.8 all-reduce.1
where the time goes:
time: 325 us; the launch traced here: 319 us
  waiting for transfers between devices  214 us (66%)
  matrix products  58.8 us (18%)
  blocking collectives  20.6 us (6%)
  between operations  13.8 us (4%)
  local copies, waits for them, and re-layouts  8.9 us (3%)
    all_gather x1, waiting for transfers between devices, shards(): lax.all_gather(weights, 'seq', axis=1, tiled=True)  106 us
    psum x1, waiting for transfers between devices, shards(): summary = lax.psum(partial_sum, 'seq')  59.8 us
    all_gather x1, waiting for transfers between devices, shards(): whole = lax.all_gather(tokens, 'head', axis=1, tiled=True)  47.6 us
    dot_general x13, matrix products, batched(): jnp.einsum('hij,hjk->hik', left, right, precision=lax.Precision.HIGHEST)  33.8 us
    all_gather x1, blocking collectives, gather_landmarks(): return lax.all_gather(local_marks, 'seq', axis=1, tiled=True)  20.6 us
    dot_general x1, matrix products, shards(): jnp.einsum('td,kdc->ktc', whole, lax.all_gather(weights, 'seq', axis=1, t...  14 us
  transfers between devices with their start and end apart: 3, of which 3 were waited for; matrix products, arithmetic and copies ran while one was open for 10% of the time, Pallas kernels for 0%

commit v1 on v0

v1 whole, which is shorter than its diff:
```python
import functools
import math

import jax
import jax.numpy as jnp
from jax import lax
from jax.experimental import pallas as pl
from jax.experimental.pallas import tpu as pltpu
from jax.sharding import PartitionSpec as P

NSTEPS = 6
TILE = 256
CHUNKS = 3
MESH = pl.DeviceIdType.MESH
BF = jnp.bfloat16
F32 = jnp.float32
NT = (((1,), (1,)), ((), ()))


def exact(left, right):
    return jnp.dot(left, right, precision=lax.Precision.HIGHEST, preferred_element_type=F32)


def row_norms(rows):
    wide = rows.astype(F32)
    square = wide * wide
    high = square.astype(BF)
    low = (square - high.astype(F32)).astype(BF)
    ones = jnp.ones((16, rows.shape[1]), BF)
    both = lax.dot_general(ones, high, NT, preferred_element_type=F32) + lax.dot_general(
        ones, low, NT, preferred_element_type=F32
    )
    return both[0:1, :]


def col_norms(rows):
    wide = rows.astype(F32)
    return jnp.sum(wide * wide, -1, keepdims=True)


def gauss(left, right):
    inner = lax.dot_general(left, right, NT, preferred_element_type=F32)
    scale = 1.0 / (2.0 * math.sqrt(left.shape[1]))
    return jnp.exp((2.0 * inner - col_norms(left) - row_norms(right)) * scale)


def kernel(
    n_head, n_seq,
    tok_ref, w_ref, pos_ref, out_ref,
    tokf, wg, acc, qkv, marks, kw, qw, part, parts_in, summ, inv, mixed, obuf,
    loc_sem, wsib_sem, ty_send, ty_recv, ts_send, ts_recv,
    up_send, up_recv, dn_send, dn_recv, x_send, x_recv,
    lm_send, lm_recv, rs_send, rs_recv, ex_send, ex_recv, ag_send, ag_recv,
    os_send, os_recv,
):
    y = lax.axis_index("head")
    s = lax.axis_index("seq")
    core = lax.rem(s, 2)
    chip = s // 2
    x = lax.rem(chip, 2)
    z = s // 4
    nz = n_seq // 4
    nch = n_seq // 2
    toks, feats = tok_ref.shape
    rows, half = w_ref.shape[1], w_ref.shape[2] // 2
    heads = pos_ref.shape[0]
    per_chip = pos_ref.shape[1]
    size = half // heads
    marks_n = per_chip * nch
    group = nch // heads
    share = marks_n // group
    sib = (y, s + 1 - 2 * core)
    xpeer = (y, s + 2 - 4 * x)
    waits = []

    def remote(src, dst, send, recv, device):
        return pltpu.make_async_remote_copy(
            src_ref=src, dst_ref=dst, send_sem=send, recv_sem=recv,
            device_id=device, device_id_type=MESH,
        )

    def chip_dev(offset):
        return (y, lax.rem(chip + offset, nch) * 2 + core)

    def head_dev(offset):
        return (lax.rem(y + offset, n_head), s)

    barrier = pltpu.get_barrier_semaphore()
    peers = [sib] + [head_dev(i) for i in range(1, n_head)] + [chip_dev(i) for i in range(1, nch)]
    for peer in peers:
        pl.semaphore_signal(barrier, inc=1, device_id=peer, device_id_type=MESH)
    pl.semaphore_wait(barrier, len(peers))

    def my_rows(seq_index):
        return pl.ds(pl.multiple_of(seq_index * rows, rows), rows)

    def half_cols(which):
        return pl.ds(pl.multiple_of(which * half, half), half)

    wsib = remote(
        w_ref.at[:, :, half_cols(1 - core)], wg.at[:, my_rows(s), :], wsib_sem.at[0],
        wsib_sem.at[1], sib,
    )
    wsib.start()
    wloc = pltpu.make_async_copy(
        w_ref.at[:, :, half_cols(core)], wg.at[:, my_rows(s), :], loc_sem.at[0]
    )
    wloc.start()
    chunk = toks // CHUNKS

    def tok_block(owner, part_index, which_core=None):
        which = core if which_core is None else which_core
        return tokf.at[
            pl.ds(pl.multiple_of(which * toks + part_index * chunk, chunk), chunk),
            pl.ds(pl.multiple_of(owner * feats, feats), feats),
        ]

    def tok_own(part_index):
        return tok_ref.at[pl.ds(part_index * chunk, chunk), :]

    for k in range(CHUNKS):
        for i in range(1, n_head):
            copy = remote(
                tok_own(k), tok_block(y, k), ty_send.at[i, k], ty_recv.at[i, k], head_dev(i)
            )
            copy.start()
            waits.append((None, copy))
    tloc = pltpu.make_async_copy(
        tok_ref,
        tokf.at[
            pl.ds(pl.multiple_of(core * toks, toks), toks),
            pl.ds(pl.multiple_of(y * feats, feats), feats),
        ],
        loc_sem.at[1],
    )
    tloc.start()
    wloc.wait()
    wsib.wait()

    for k in range(CHUNKS):
        copy = remote(tok_own(k), tok_block(y, k), ts_send.at[0, k], ts_recv.at[0, k], sib)
        copy.start()
        waits.append((None, copy))

    def block(phase, zb, xb):
        which = pl.ds(0, 2) if phase == 0 else pl.ds(2, 1)
        at = pl.multiple_of((zb * 2 + xb) * 2 * rows, 2 * rows)
        return wg.at[which, pl.ds(at, 2 * rows), :]

    def guarded(condition, copy_of):
        @pl.when(condition)
        def _():
            copy_of().start()

        waits.append((condition, copy_of))

    def up(phase, t):
        def copy():
            ref = block(phase, z - t, x)
            return remote(ref, ref, up_send.at[phase, t], up_recv.at[phase, t], (y, s + 4))

        return copy

    def down(phase, t):
        def copy():
            ref = block(phase, z + t, x)
            return remote(ref, ref, dn_send.at[phase, t], dn_recv.at[phase, t], (y, s - 4))

        return copy

    def across(phase, zb):
        def copy():
            ref = block(phase, zb, x)
            return remote(ref, ref, x_send.at[phase, zb], x_recv.at[phase, zb], xpeer)

        return copy

    def from_below(phase, t):
        ref = block(phase, z - 1 - t, x)
        return remote(ref, ref, up_send.at[phase, t], up_recv.at[phase, t], (y, s - 4))

    def from_above(phase, t):
        ref = block(phase, z + 1 + t, x)
        return remote(ref, ref, dn_send.at[phase, t], dn_recv.at[phase, t], (y, s + 4))

    def line_start(phase):
        guarded(z + 1 < nz, up(phase, 0))
        guarded(z >= 1, down(phase, 0))
        copy = across(phase, z)()
        copy.start()
        waits.append((None, copy))

    def line_step(phase, t):
        below = z - 1 - t >= 0
        above = z + 1 + t < nz

        @pl.when(below)
        def _():
            from_below(phase, t).wait_recv()

        if t + 1 < nz - 1:
            guarded(below & (z + 1 < nz), up(phase, t + 1))
        guarded(below, across(phase, z - 1 - t))

        @pl.when(above)
        def _():
            from_above(phase, t).wait_recv()

        if t + 1 < nz - 1:
            guarded(above & (z >= 1), down(phase, t + 1))
        guarded(above, across(phase, z + 1 + t))

    def across_wait(phase, zb):
        ref = block(phase, zb, 1 - x)
        remote(ref, ref, x_send.at[phase, zb], x_recv.at[phase, zb], xpeer).wait_recv()

    def forward_tokens(k):
        for i in range(1, n_head):
            owner = lax.rem(y + n_head - i, n_head)
            ref = tok_block(owner, k)
            remote(ref, ref, ty_send.at[i, k], ty_recv.at[i, k], head_dev(n_head - i)).wait_recv()
            copy = remote(ref, ref, ts_send.at[i, k], ts_recv.at[i, k], sib)
            copy.start()
            waits.append((None, copy))

    line_start(0)
    for t in range(nz - 1):
        line_step(0, t)
        if t < CHUNKS:
            forward_tokens(t)
    for k in range(nz - 1, CHUNKS):
        forward_tokens(k)
    line_start(1)
    tloc.wait()
    for i in range(n_head):
        owner = lax.rem(y + n_head - i, n_head)
        for k in range(CHUNKS):
            ref = tok_block(owner, k, 1 - core)
            remote(ref, ref, ts_send.at[i, k], ts_recv.at[i, k], sib).wait_recv()

    order = [jnp.where(z < nz // 2, i, nz - 1 - i) for i in range(nz)]
    near, far = order[: nz - nz // 4], order[nz - nz // 4 :]
    deep = 4 * rows

    def project(p, blocks, last):
        def body(i, carry):
            at = pl.ds(pl.multiple_of(i * TILE, TILE), TILE)
            total = None
            for zb in blocks:
                inner = pl.ds(pl.multiple_of(zb * deep, deep), deep)
                term = jnp.dot(tokf[at, inner], wg[p, inner, :], preferred_element_type=F32)
                total = term if total is None else total + term
            if last:
                qkv[p, at, :] = (acc[p, at, :] + total).astype(BF)
            else:
                acc[p, at, :] = total
            return carry

        lax.fori_loop(0, 2 * toks // TILE, body, 0)

    for zb in near:
        across_wait(0, zb)
    project(0, near, False)
    line_step(1, 0)
    project(1, near, False)
    for zb in far:
        across_wait(0, zb)
    project(0, far, True)
    project(1, far, True)
    for t in range(1, nz - 1):
        line_step(1, t)

    def cols(h):
        return pl.ds(h * size, size)

    places = lax.broadcasted_iota(jnp.int32, (per_chip, 2 * toks), 1)
    even = lax.broadcasted_iota(jnp.int32, (per_chip, size), 0) % 2 == 0
    for h in range(heads):
        picker = jnp.where(places == pos_ref[h], 1.0, 0.0).astype(BF)
        picked_q = jnp.dot(picker, qkv[0, :, cols(h)], preferred_element_type=F32)
        picked_k = jnp.dot(picker, qkv[1, :, cols(h)], preferred_element_type=F32)
        marks[chip, h] = jnp.where(even, picked_q, picked_k).astype(BF)

    def all_chips(source, buffer, send, recv, index=lambda offset: chip):
        for i in range(1, nch):
            copy = remote(source(i), buffer, send.at[i], recv.at[i], chip_dev(i))
            copy.start()
            waits.append((None, copy))

    def from_chips(buffer, send, recv):
        for i in range(1, nch):
            ref = buffer.at[lax.rem(chip + nch - i, nch)]
            remote(ref, ref, send.at[i], recv.at[i], chip_dev(nch - i)).wait_recv()

    all_chips(lambda i: marks.at[chip], marks.at[chip], lm_send, lm_recv)
    from_chips(marks, lm_send, lm_recv)

    def marks_of(h):
        return marks[:, h].astype(F32).reshape(marks_n, size).astype(BF)

    for h in range(heads):
        own = marks_of(h)

        def weigh(i, carry):
            at = pl.ds(pl.multiple_of(i * TILE, TILE), TILE)
            kw[h, :, at] = gauss(own, qkv[1, at, cols(h)]).astype(BF)
            return carry

        lax.fori_loop(0, 2 * toks // TILE, weigh, 0)

    mine = marks_of(chip // group)
    inner = gauss(mine, mine)
    scale_cols = jnp.max(jnp.sum(jnp.abs(inner), 0, keepdims=True))
    scale_rows = jnp.max(jnp.sum(jnp.abs(inner), 1, keepdims=True))
    iterate = inner / (scale_cols * scale_rows)
    for step in range(NSTEPS):
        iterate = 2.0 * iterate - exact(exact(iterate, inner), iterate)
    inv[...] = iterate

    for zb in near:
        across_wait(1, zb)
    project(2, near, False)
    for zb in far:
        across_wait(1, zb)
    project(2, far, True)

    for h in range(heads):
        total = jnp.dot(kw[h], qkv[2, :, cols(h)], preferred_element_type=F32)
        for j in range(group):
            part[h * group + j] = total[j * share : (j + 1) * share]
    all_chips(
        lambda i: part.at[lax.rem(chip + i, nch)], parts_in.at[chip], rs_send, rs_recv
    )
    for h in range(heads):
        own = marks_of(h)

        def weigh_q(i, carry):
            at = pl.ds(pl.multiple_of(i * TILE, TILE), TILE)
            qw[h, at, :] = gauss(qkv[0, at, cols(h)], own).astype(BF)
            return carry

        lax.fori_loop(0, 2 * toks // TILE, weigh_q, 0)
    from_chips(parts_in, rs_send, rs_recv)
    total = part[chip]
    for i in range(1, nch):
        total = total + parts_in[lax.rem(chip + i, nch)]
    member = lax.rem(chip, group)
    base = chip - member
    summ[member] = total

    def mate(i):
        return lax.rem(member + i, group)

    for i in range(1, group):
        ref = summ.at[member]
        copy = remote(ref, ref, ex_send.at[i], ex_recv.at[i], (y, (base + mate(i)) * 2 + core))
        copy.start()
        waits.append((None, copy))
    for i in range(1, group):
        source = mate(group - i)
        ref = summ.at[source]
        remote(ref, ref, ex_send.at[i], ex_recv.at[i], (y, (base + source) * 2 + core)).wait_recv()
    some = inv[pl.ds(pl.multiple_of(member * share, share), share), :]
    mixed[chip] = exact(some, summ[...].reshape(marks_n, size)).astype(BF)
    all_chips(lambda i: mixed.at[chip], mixed.at[chip], ag_send, ag_recv)
    from_chips(mixed, ag_send, ag_recv)

    own_at = pl.ds(pl.multiple_of(core * toks, toks), toks)
    sib_at = pl.ds(pl.multiple_of((1 - core) * toks, toks), toks)
    for h in range(heads):
        values = jnp.concatenate(
            [mixed[h * group + j].astype(F32) for j in range(group)], axis=0
        ).astype(BF)
        obuf[h] = jnp.dot(qw[h, sib_at, :], values, preferred_element_type=F32).astype(BF)
        where = pl.ds(pl.multiple_of(core * half + h * size, size), size)
        copy = remote(obuf.at[h], out_ref.at[:, where], os_send.at[h], os_recv.at[h], sib)
        copy.start()
        waits.append((None, copy))
        out_ref[:, where] = jnp.dot(
            qw[h, own_at, :], values, preferred_element_type=F32
        ).astype(BF)
    for h in range(heads):
        where = pl.ds(pl.multiple_of((1 - core) * half + h * size, size), size)
        remote(obuf.at[h], out_ref.at[:, where], os_send.at[h], os_recv.at[h], sib).wait_recv()

    for condition, copy in waits:
        if condition is None:
            copy.wait_send()
        else:
            pl.when(condition)(lambda: copy().wait_send())


def shards(tokens, weights, landmark_pos, n_head, n_seq):
    toks, feats = tokens.shape
    _, rows, wide = weights.shape
    heads = landmark_pos.shape[0] // 2
    marks_n = landmark_pos.shape[1]
    half = wide // 2
    size = half // heads
    nch, nz = n_seq // 2, n_seq // 4
    per_chip = marks_n // nch
    group = nch // heads
    share = marks_n // group
    s = lax.axis_index("seq")
    chip, core = s // 2, lax.rem(s, 2)
    pos = lax.dynamic_slice(landmark_pos, (core * heads, chip * per_chip), (heads, per_chip))
    pos = (pos - chip * (2 * toks))[:, :, None]
    dma = pltpu.SemaphoreType.DMA
    vmem = pl.BlockSpec(memory_space=pltpu.VMEM)
    return pl.pallas_call(
        functools.partial(kernel, n_head, n_seq),
        out_shape=jax.ShapeDtypeStruct((toks, wide), BF),
        in_specs=[vmem] * 3,
        out_specs=vmem,
        scratch_shapes=[
            pltpu.VMEM((2 * toks, n_head * feats), BF),
            pltpu.VMEM((3, n_seq * rows, half), BF),
            pltpu.VMEM((3, 2 * toks, half), F32),
            pltpu.VMEM((3, 2 * toks, half), BF),
            pltpu.VMEM((nch, heads, per_chip, size), BF),
            pltpu.VMEM((heads, marks_n, 2 * toks), BF),
            pltpu.VMEM((heads, 2 * toks, marks_n), BF),
            pltpu.VMEM((nch, share, size), F32),
            pltpu.VMEM((nch, share, size), F32),
            pltpu.VMEM((group, share, size), F32),
            pltpu.VMEM((marks_n, marks_n), F32),
            pltpu.VMEM((nch, share, size), BF),
            pltpu.VMEM((heads, toks, size), BF),
            dma((2,)), dma((2,)),
            dma((n_head, CHUNKS)), dma((n_head, CHUNKS)),
            dma((n_head, CHUNKS)), dma((n_head, CHUNKS)),
            dma((2, nz - 1)), dma((2, nz - 1)), dma((2, nz - 1)), dma((2, nz - 1)),
            dma((2, nz)), dma((2, nz)),
            dma((nch,)), dma((nch,)), dma((nch,)), dma((nch,)),
            dma((group,)), dma((group,)), dma((nch,)), dma((nch,)),
            dma((heads,)), dma((heads,)),
        ],
        compiler_params=pltpu.CompilerParams(
            collective_id=0, has_side_effects=True, vmem_limit_bytes=56 * 2**20
        ),
    )(tokens, weights, pos)


def solution(mesh):
    return jax.shard_map(
        functools.partial(shards, n_head=mesh.shape["head"], n_seq=mesh.shape["seq"]),
        mesh=mesh,
        in_specs=(P("seq", "head"), P(None, "seq", "head"), P("head", None)),
        out_specs=P("seq", "head"),
        check_vma=False,
    )
```

time: 325 us -> 132 us (0.41); the launches traced: 319 us -> 132 us
  waiting for transfers between devices: 214 us -> 0 us
  Pallas kernels: 0 us -> 128 us
  matrix products: 58.8 us -> 0 us
  blocking collectives: 20.6 us -> 0 us
  between operations: 13.8 us -> 0.01 us
  local copies, waits for them, and re-layouts: 8.9 us -> 3.41 us
    all_gather x2 -> x0, waiting for transfers between devices: 154 us -> none  [the longest x1 106 us: shards(): lax.all_gather(weights, 'seq', axis=1, tiled=True)]
    pallas_call x0 -> x1, Pallas kernels: none -> 128 us  [shards(): pl.pallas_call(functools.partial(kernel, n_head, n_seq), out_shape=jax.Sh...]
    psum x1 -> x0, waiting for transfers between devices: 59.8 us -> none  [shards(): summary = lax.psum(partial_sum, 'seq')]
    dot_general x19 -> x0, matrix products: 58.8 us -> none  [the longest x13 33.8 us: batched(): jnp.einsum('hij,hjk->hik', left, right, precision=lax.Precision.HIGHEST)]
    all_gather x1 -> x0, blocking collectives: 20.6 us -> none  [gather_landmarks(): return lax.all_gather(local_marks, 'seq', axis=1, tiled=True)]
    convert_element_type x3 -> x0, local copies, waits for them, and re-layouts: 5.38 us -> none  [the longest x2 2.81 us: heads_of(): flat.astype(jnp.bfloat16).reshape(tok_rows, heads_dev, head_size)]
  transfers between devices with their start and end apart: 3 -> 0, of which waited for: 3 -> 0; matrix products, arithmetic and copies ran while one was open for 10% -> 0% of each run, Pallas kernels for 0% -> 0%
where the time goes in v1:
time: 132 us
  Pallas kernels  128 us (97%)
  local copies, waits for them, and re-layouts  3.41 us (3%)
    pallas_call x1, Pallas kernels, shards(): pl.pallas_call(functools.partial(kernel, n_head, n_seq), out_shape=jax.Sh...  128 us
    unnamed x1, local copies, waits for them, and re-layouts  2.67 us

profile of v1, /device:TPU:0, one launch (start us, length us, event | category | flops | bytes accessed | tf_op | source)
XLA Modules:
  0.0 132.1 jit_solution(5103799370485944250)
XLA Ops:
  0.0 0.8 subtract_bitcast_fusion
  0.8 0.7 copy.4.pos_ref
  1.5 127.9 %shard_map.37 = bf16[768,1024]{1,0:T(8,128)(2,1)} custom-call(bf16[768,1024]{1,0:T(8,128)(2,1)} %tok_ref.1, bf16[3,128,1024]{2,1,0:T(8,128)(2,1)} %w_ref.1, s32[4,32,1]{2,1,0:T(8,128)} %copy.4.pos_ref), custom_call_target="tpu_custom_call" | custom-call | tf_op jit(solution)/shard_map/pallas_call | solution.py:410
  129.4 2.7 %copy.6 = bf16[768,1024]{1,0:T(8,128)(2,1)} copy(bf16[768,1024]{1,0:T(8,128)(2,1)} %shard_map.37) | data formatting | bytes 3145728

commit v2 on v1

--- a/solution.py
+++ b/solution.py
@@ -49,7 +49,7 @@
     tok_ref, w_ref, pos_ref, out_ref,
     tokf, wg, acc, qkv, marks, kw, qw, part, parts_in, summ, inv, mixed, obuf,
     loc_sem, wsib_sem, ty_send, ty_recv, ts_send, ts_recv,
-    up_send, up_recv, dn_send, dn_recv, x_send, x_recv,
+    up_send, up_recv, dn_send, dn_recv, x_send, x_recv, near_send, near_recv,
     lm_send, lm_recv, rs_send, rs_recv, ex_send, ex_recv, ag_send, ag_recv,
     os_send, os_recv,
 ):
@@ -63,10 +63,9 @@
     nch = n_seq // 2
     toks, feats = tok_ref.shape
     rows, half = w_ref.shape[1], w_ref.shape[2] // 2
-    heads = pos_ref.shape[0]
-    per_chip = pos_ref.shape[1]
+    heads, marks_n = pos_ref.shape[0] // 2, pos_ref.shape[1]
+    per_chip = marks_n // nch
     size = half // heads
-    marks_n = per_chip * nch
     group = nch // heads
     share = marks_n // group
     sib = (y, s + 1 - 2 * core)
@@ -143,9 +142,8 @@
         waits.append((None, copy))
 
     def block(phase, zb, xb):
-        which = pl.ds(0, 2) if phase == 0 else pl.ds(2, 1)
         at = pl.multiple_of((zb * 2 + xb) * 2 * rows, 2 * rows)
-        return wg.at[which, pl.ds(at, 2 * rows), :]
+        return wg.at[phase, pl.ds(at, 2 * rows), :]
 
     def guarded(condition, copy_of):
         @pl.when(condition)
@@ -200,7 +198,8 @@
 
         if t + 1 < nz - 1:
             guarded(below & (z + 1 < nz), up(phase, t + 1))
-        guarded(below, across(phase, z - 1 - t))
+        if phase < 2 or t > 0:
+            guarded(below, across(phase, z - 1 - t))
 
         @pl.when(above)
         def _():
@@ -208,7 +207,8 @@
 
         if t + 1 < nz - 1:
             guarded(above & (z >= 1), down(phase, t + 1))
-        guarded(above, across(phase, z + 1 + t))
+        if phase < 2 or t > 0:
+            guarded(above, across(phase, z + 1 + t))
 
     def across_wait(phase, zb):
         ref = block(phase, zb, 1 - x)
@@ -224,13 +224,15 @@
             waits.append((None, copy))
 
     line_start(0)
+    line_start(1)
     for t in range(nz - 1):
         line_step(0, t)
+        line_step(1, t)
         if t < CHUNKS:
             forward_tokens(t)
     for k in range(nz - 1, CHUNKS):
         forward_tokens(k)
-    line_start(1)
+    line_start(2)
     tloc.wait()
     for i in range(n_head):
         owner = lax.rem(y + n_head - i, n_head)
@@ -258,30 +260,50 @@
 
         lax.fori_loop(0, 2 * toks // TILE, body, 0)
 
+    def neighbour(step, plane):
+        ref = block(2, plane, 1 - x)
+        way = (step + 1) // 2
+        return remote(ref, ref, near_send.at[way], near_recv.at[way], (y, s + 4 * step))
+
+    def values_wait(zb):
+        pl.when(zb == z - 1)(lambda: neighbour(1, z - 1).wait_recv())
+        pl.when(zb == z + 1)(lambda: neighbour(-1, z + 1).wait_recv())
+        pl.when((zb < z - 1) | (zb > z + 1))(lambda: across_wait(2, zb))
+
     for zb in near:
         across_wait(0, zb)
     project(0, near, False)
-    line_step(1, 0)
+    line_step(2, 0)
+    for zb in near:
+        across_wait(1, zb)
     project(1, near, False)
+    for t in range(1, nz - 1):
+        line_step(2, t)
     for zb in far:
         across_wait(0, zb)
     project(0, far, True)
+    for zb in far:
+        across_wait(1, zb)
     project(1, far, True)
-    for t in range(1, nz - 1):
-        line_step(1, t)
 
     def cols(h):
         return pl.ds(h * size, size)
 
     places = lax.broadcasted_iota(jnp.int32, (per_chip, 2 * toks), 1)
     even = lax.broadcasted_iota(jnp.int32, (per_chip, size), 0) % 2 == 0
-    for h in range(heads):
-        picker = jnp.where(places == pos_ref[h], 1.0, 0.0).astype(BF)
+    own_mark = lax.broadcasted_iota(jnp.int32, (per_chip, marks_n), 1) == (
+        chip * per_chip + lax.broadcasted_iota(jnp.int32, (per_chip, marks_n), 0)
+    )
+    first = chip * (2 * toks)
+    for h in range(heads):
+        head_pos = pos_ref[pl.ds(core * heads + h, 1), :]
+        place = jnp.sum(jnp.where(own_mark, head_pos, 0), -1, keepdims=True) - first
+        picker = jnp.where(places == place, 1.0, 0.0).astype(BF)
         picked_q = jnp.dot(picker, qkv[0, :, cols(h)], preferred_element_type=F32)
         picked_k = jnp.dot(picker, qkv[1, :, cols(h)], preferred_element_type=F32)
         marks[chip, h] = jnp.where(even, picked_q, picked_k).astype(BF)
 
-    def all_chips(source, buffer, send, recv, index=lambda offset: chip):
+    def all_chips(source, buffer, send, recv):
         for i in range(1, nch):
             copy = remote(source(i), buffer, send.at[i], recv.at[i], chip_dev(i))
             copy.start()
@@ -293,6 +315,12 @@
             remote(ref, ref, send.at[i], recv.at[i], chip_dev(nch - i)).wait_recv()
 
     all_chips(lambda i: marks.at[chip], marks.at[chip], lm_send, lm_recv)
+    across_wait(2, z)
+    guarded(z + 1 < nz, lambda: neighbour(1, z))
+    guarded(z >= 1, lambda: neighbour(-1, z))
+    for zb in near:
+        values_wait(zb)
+    project(2, near, False)
     from_chips(marks, lm_send, lm_recv)
 
     def marks_of(h):
@@ -308,6 +336,17 @@
 
         lax.fori_loop(0, 2 * toks // TILE, weigh, 0)
 
+    for zb in far:
+        values_wait(zb)
+    project(2, far, True)
+
+    for h in range(heads):
+        total = jnp.dot(kw[h], qkv[2, :, cols(h)], preferred_element_type=F32)
+        for j in range(group):
+            part[h * group + j] = total[j * share : (j + 1) * share]
+    all_chips(
+        lambda i: part.at[lax.rem(chip + i, nch)], parts_in.at[chip], rs_send, rs_recv
+    )
     mine = marks_of(chip // group)
     inner = gauss(mine, mine)
     scale_cols = jnp.max(jnp.sum(jnp.abs(inner), 0, keepdims=True))
@@ -317,20 +356,6 @@
         iterate = 2.0 * iterate - exact(exact(iterate, inner), iterate)
     inv[...] = iterate
 
-    for zb in near:
-        across_wait(1, zb)
-    project(2, near, False)
-    for zb in far:
-        across_wait(1, zb)
-    project(2, far, True)
-
-    for h in range(heads):
-        total = jnp.dot(kw[h], qkv[2, :, cols(h)], preferred_element_type=F32)
-        for j in range(group):
-            part[h * group + j] = total[j * share : (j + 1) * share]
-    all_chips(
-        lambda i: part.at[lax.rem(chip + i, nch)], parts_in.at[chip], rs_send, rs_recv
-    )
     for h in range(heads):
         own = marks_of(h)
 
@@ -360,17 +385,25 @@
         source = mate(group - i)
         ref = summ.at[source]
         remote(ref, ref, ex_send.at[i], ex_recv.at[i], (y, (base + source) * 2 + core)).wait_recv()
-    some = inv[pl.ds(pl.multiple_of(member * share, share), share), :]
-    mixed[chip] = exact(some, summ[...].reshape(marks_n, size)).astype(BF)
-    all_chips(lambda i: mixed.at[chip], mixed.at[chip], ag_send, ag_recv)
-    from_chips(mixed, ag_send, ag_recv)
+    owned = chip // group
+    mixed[owned] = exact(inv[...], summ[...].reshape(marks_n, size)).astype(BF)
+
+    def like(offset):
+        return (y, (lax.rem(owned + offset, heads) * group + member) * 2 + core)
+
+    for i in range(1, heads):
+        ref = mixed.at[owned]
+        copy = remote(ref, ref, ag_send.at[i], ag_recv.at[i], like(i))
+        copy.start()
+        waits.append((None, copy))
+    for i in range(1, heads):
+        ref = mixed.at[lax.rem(owned + heads - i, heads)]
+        remote(ref, ref, ag_send.at[i], ag_recv.at[i], like(heads - i)).wait_recv()
 
     own_at = pl.ds(pl.multiple_of(core * toks, toks), toks)
     sib_at = pl.ds(pl.multiple_of((1 - core) * toks, toks), toks)
     for h in range(heads):
-        values = jnp.concatenate(
-            [mixed[h * group + j].astype(F32) for j in range(group)], axis=0
-        ).astype(BF)
+        values = mixed[h]
         obuf[h] = jnp.dot(qw[h, sib_at, :], values, preferred_element_type=F32).astype(BF)
         where = pl.ds(pl.multiple_of(core * half + h * size, size), size)
         copy = remote(obuf.at[h], out_ref.at[:, where], os_send.at[h], os_recv.at[h], sib)
@@ -401,10 +434,6 @@
     per_chip = marks_n // nch
     group = nch // heads
     share = marks_n // group
-    s = lax.axis_index("seq")
-    chip, core = s // 2, lax.rem(s, 2)
-    pos = lax.dynamic_slice(landmark_pos, (core * heads, chip * per_chip), (heads, per_chip))
-    pos = (pos - chip * (2 * toks))[:, :, None]
     dma = pltpu.SemaphoreType.DMA
     vmem = pl.BlockSpec(memory_space=pltpu.VMEM)
     return pl.pallas_call(
@@ -424,21 +453,21 @@
             pltpu.VMEM((nch, share, size), F32),
             pltpu.VMEM((group, share, size), F32),
             pltpu.VMEM((marks_n, marks_n), F32),
-            pltpu.VMEM((nch, share, size), BF),
+            pltpu.VMEM((heads, marks_n, size), BF),
             pltpu.VMEM((heads, toks, size), BF),
             dma((2,)), dma((2,)),
             dma((n_head, CHUNKS)), dma((n_head, CHUNKS)),
             dma((n_head, CHUNKS)), dma((n_head, CHUNKS)),
-            dma((2, nz - 1)), dma((2, nz - 1)), dma((2, nz - 1)), dma((2, nz - 1)),
-            dma((2, nz)), dma((2, nz)),
+            dma((3, nz - 1)), dma((3, nz - 1)), dma((3, nz - 1)), dma((3, nz - 1)),
+            dma((3, nz)), dma((3, nz)), dma((2,)), dma((2,)),
             dma((nch,)), dma((nch,)), dma((nch,)), dma((nch,)),
-            dma((group,)), dma((group,)), dma((nch,)), dma((nch,)),
+            dma((group,)), dma((group,)), dma((heads,)), dma((heads,)),
             dma((heads,)), dma((heads,)),
         ],
         compiler_params=pltpu.CompilerParams(
             collective_id=0, has_side_effects=True, vmem_limit_bytes=56 * 2**20
         ),
-    )(tokens, weights, pos)
+    )(tokens, weights, landmark_pos)
 
 
 def solution(mesh):

time: 132 us -> 117 us (0.89)
  Pallas kernels: 128 us -> 115 us
    pallas_call x1, Pallas kernels: 128 us -> 115 us  [shards(): pl.pallas_call(functools.partial(kernel, n_head, n_seq), out_shape=jax.Sh...]
where the time goes in v2:
time: 117 us
  Pallas kernels  115 us (98%)
  local copies, waits for them, and re-layouts  2.67 us (2%)
    pallas_call x1, Pallas kernels, shards(): pl.pallas_call(functools.partial(kernel, n_head, n_seq), out_shape=jax.Sh...  115 us
    unnamed x1, local copies, waits for them, and re-layouts  2.67 us

profile of v2, /device:TPU:0, one launch (start us, length us, event | category | flops | bytes accessed | tf_op | source)
XLA Modules:
  0.0 117.3 jit_solution(12308422670236272716)
XLA Ops:
  0.0 114.6 %shard_map.37 = bf16[768,1024]{1,0:T(8,128)(2,1)} custom-call(bf16[768,1024]{1,0:T(8,128)(2,1)} %tok_ref.1, bf16[3,128,1024]{2,1,0:T(8,128)(2,1)} %w_ref.1, s32[8,256]{1,0:T(8,128)} %pos_ref.1), custom_call_target="tpu_custom_call" | custom-call | tf_op jit(solution)/shard_map/pallas_call | solution.py:439
  114.7 2.7 %copy.5 = bf16[768,1024]{1,0:T(8,128)(2,1)} copy(bf16[768,1024]{1,0:T(8,128)(2,1)} %shard_map.37) | data formatting | bytes 3145728

commit v3 on v2

--- a/solution.py
+++ b/solution.py
@@ -96,15 +96,19 @@
     def half_cols(which):
         return pl.ds(pl.multiple_of(which * half, half), half)
 
-    wsib = remote(
-        w_ref.at[:, :, half_cols(1 - core)], wg.at[:, my_rows(s), :], wsib_sem.at[0],
-        wsib_sem.at[1], sib,
-    )
-    wsib.start()
-    wloc = pltpu.make_async_copy(
-        w_ref.at[:, :, half_cols(core)], wg.at[:, my_rows(s), :], loc_sem.at[0]
-    )
-    wloc.start()
+    wsib, wloc = [], []
+    for p in range(3):
+        copy = remote(
+            w_ref.at[p, :, half_cols(1 - core)], wg.at[p, my_rows(s), :], wsib_sem.at[0, p],
+            wsib_sem.at[1, p], sib,
+        )
+        copy.start()
+        wsib.append(copy)
+        copy = pltpu.make_async_copy(
+            w_ref.at[p, :, half_cols(core)], wg.at[p, my_rows(s), :], loc_sem.at[p]
+        )
+        copy.start()
+        wloc.append(copy)
     chunk = toks // CHUNKS
 
     def tok_block(owner, part_index, which_core=None):
@@ -130,17 +134,9 @@
             pl.ds(pl.multiple_of(core * toks, toks), toks),
             pl.ds(pl.multiple_of(y * feats, feats), feats),
         ],
-        loc_sem.at[1],
+        loc_sem.at[3],
     )
     tloc.start()
-    wloc.wait()
-    wsib.wait()
-
-    for k in range(CHUNKS):
-        copy = remote(tok_own(k), tok_block(y, k), ts_send.at[0, k], ts_recv.at[0, k], sib)
-        copy.start()
-        waits.append((None, copy))
-
     def block(phase, zb, xb):
         at = pl.multiple_of((zb * 2 + xb) * 2 * rows, 2 * rows)
         return wg.at[phase, pl.ds(at, 2 * rows), :]
@@ -182,6 +178,8 @@
         return remote(ref, ref, dn_send.at[phase, t], dn_recv.at[phase, t], (y, s + 4))
 
     def line_start(phase):
+        wloc[phase].wait()
+        wsib[phase].wait()
         guarded(z + 1 < nz, up(phase, 0))
         guarded(z >= 1, down(phase, 0))
         copy = across(phase, z)()
@@ -225,14 +223,16 @@
 
     line_start(0)
     line_start(1)
+    for k in range(CHUNKS):
+        copy = remote(tok_own(k), tok_block(y, k), ts_send.at[0, k], ts_recv.at[0, k], sib)
+        copy.start()
+        waits.append((None, copy))
     for t in range(nz - 1):
         line_step(0, t)
         line_step(1, t)
-        if t < CHUNKS:
-            forward_tokens(t)
-    for k in range(nz - 1, CHUNKS):
+    line_start(2)
+    for k in range(CHUNKS):
         forward_tokens(k)
-    line_start(2)
     tloc.wait()
     for i in range(n_head):
         owner = lax.rem(y + n_head - i, n_head)
@@ -403,14 +403,15 @@
     own_at = pl.ds(pl.multiple_of(core * toks, toks), toks)
     sib_at = pl.ds(pl.multiple_of((1 - core) * toks, toks), toks)
     for h in range(heads):
-        values = mixed[h]
-        obuf[h] = jnp.dot(qw[h, sib_at, :], values, preferred_element_type=F32).astype(BF)
+        obuf[h] = jnp.dot(qw[h, sib_at, :], mixed[h], preferred_element_type=F32).astype(BF)
         where = pl.ds(pl.multiple_of(core * half + h * size, size), size)
         copy = remote(obuf.at[h], out_ref.at[:, where], os_send.at[h], os_recv.at[h], sib)
         copy.start()
         waits.append((None, copy))
+    for h in range(heads):
+        where = pl.ds(pl.multiple_of(core * half + h * size, size), size)
         out_ref[:, where] = jnp.dot(
-            qw[h, own_at, :], values, preferred_element_type=F32
+            qw[h, own_at, :], mixed[h], preferred_element_type=F32
         ).astype(BF)
     for h in range(heads):
         where = pl.ds(pl.multiple_of((1 - core) * half + h * size, size), size)
@@ -455,7 +456,7 @@
             pltpu.VMEM((marks_n, marks_n), F32),
             pltpu.VMEM((heads, marks_n, size), BF),
             pltpu.VMEM((heads, toks, size), BF),
-            dma((2,)), dma((2,)),
+            dma((4,)), dma((2, 3)),
             dma((n_head, CHUNKS)), dma((n_head, CHUNKS)),
             dma((n_head, CHUNKS)), dma((n_head, CHUNKS)),
             dma((3, nz - 1)), dma((3, nz - 1)), dma((3, nz - 1)), dma((3, nz - 1)),

time: 117 us -> 117 us (level)
  no operation moved by 1% of the time
where the time goes in v3:
time: 117 us
  Pallas kernels  114 us (97%)
  local copies, waits for them, and re-layouts  2.67 us (2%)
    pallas_call x1, Pallas kernels, shards(): pl.pallas_call(functools.partial(kernel, n_head, n_seq), out_shape=jax.Sh...  114 us
    unnamed x1, local copies, waits for them, and re-layouts  2.67 us

profile of v3, /device:TPU:0, one launch (start us, length us, event | category | flops | bytes accessed | tf_op | source)
XLA Modules:
  0.0 116.9 jit_solution(10856060776851328034)
XLA Ops:
  0.0 114.2 %shard_map.37 = bf16[768,1024]{1,0:T(8,128)(2,1)} custom-call(bf16[768,1024]{1,0:T(8,128)(2,1)} %tok_ref.1, bf16[3,128,1024]{2,1,0:T(8,128)(2,1)} %w_ref.1, s32[8,256]{1,0:T(8,128)} %pos_ref.1), custom_call_target="tpu_custom_call" | custom-call | tf_op jit(solution)/shard_map/pallas_call | solution.py:440
  114.2 2.7 %copy.5 = bf16[768,1024]{1,0:T(8,128)(2,1)} copy(bf16[768,1024]{1,0:T(8,128)(2,1)} %shard_map.37) | data formatting | bytes 3145728

commit v4 on v3

--- a/solution.py
+++ b/solution.py
@@ -47,7 +47,7 @@
 def kernel(
     n_head, n_seq,
     tok_ref, w_ref, pos_ref, out_ref,
-    tokf, wg, acc, qkv, marks, kw, qw, part, parts_in, summ, inv, mixed, obuf,
+    tokf, wg, acc, qkv, marks, kw, qw, part, parts_in, own_part, summ, inv, mixed, obuf,
     loc_sem, wsib_sem, ty_send, ty_recv, ts_send, ts_recv,
     up_send, up_recv, dn_send, dn_recv, x_send, x_recv, near_send, near_recv,
     lm_send, lm_recv, rs_send, rs_recv, ex_send, ex_recv, ag_send, ag_recv,
@@ -336,17 +336,6 @@
 
         lax.fori_loop(0, 2 * toks // TILE, weigh, 0)
 
-    for zb in far:
-        values_wait(zb)
-    project(2, far, True)
-
-    for h in range(heads):
-        total = jnp.dot(kw[h], qkv[2, :, cols(h)], preferred_element_type=F32)
-        for j in range(group):
-            part[h * group + j] = total[j * share : (j + 1) * share]
-    all_chips(
-        lambda i: part.at[lax.rem(chip + i, nch)], parts_in.at[chip], rs_send, rs_recv
-    )
     mine = marks_of(chip // group)
     inner = gauss(mine, mine)
     scale_cols = jnp.max(jnp.sum(jnp.abs(inner), 0, keepdims=True))
@@ -356,6 +345,29 @@
         iterate = 2.0 * iterate - exact(exact(iterate, inner), iterate)
     inv[...] = iterate
 
+    for zb in far:
+        values_wait(zb)
+    project(2, far, True)
+
+    def share_out(target):
+        return remote(
+            part.at[target], parts_in.at[chip], rs_send.at[target], rs_recv.at[chip],
+            (y, target * 2 + core),
+        )
+
+    for h in range(heads):
+        total = jnp.dot(kw[h], qkv[2, :, cols(h)], preferred_element_type=F32)
+        for j in range(group):
+            target = h * group + j
+            piece = total[j * share : (j + 1) * share]
+
+            @pl.when(target == chip)
+            def _():
+                own_part[...] = piece
+
+            part[target] = piece.astype(BF)
+            guarded(target != chip, lambda target=target: share_out(target))
+
     for h in range(heads):
         own = marks_of(h)
 
@@ -365,10 +377,13 @@
             return carry
 
         lax.fori_loop(0, 2 * toks // TILE, weigh_q, 0)
-    from_chips(parts_in, rs_send, rs_recv)
-    total = part[chip]
     for i in range(1, nch):
-        total = total + parts_in[lax.rem(chip + i, nch)]
+        source = lax.rem(chip + i, nch)
+        ref = parts_in.at[source]
+        remote(ref, ref, rs_send.at[source], rs_recv.at[source], chip_dev(i)).wait_recv()
+    total = own_part[...]
+    for i in range(1, nch):
+        total = total + parts_in[lax.rem(chip + i, nch)].astype(F32)
     member = lax.rem(chip, group)
     base = chip - member
     summ[member] = total
@@ -450,8 +465,9 @@
             pltpu.VMEM((nch, heads, per_chip, size), BF),
             pltpu.VMEM((heads, marks_n, 2 * toks), BF),
             pltpu.VMEM((heads, 2 * toks, marks_n), BF),
-            pltpu.VMEM((nch, share, size), F32),
-            pltpu.VMEM((nch, share, size), F32),
+            pltpu.VMEM((nch, share, size), BF),
+            pltpu.VMEM((nch, share, size), BF),
+            pltpu.VMEM((share, size), F32),
             pltpu.VMEM((group, share, size), F32),
             pltpu.VMEM((marks_n, marks_n), F32),
             pltpu.VMEM((heads, marks_n, size), BF),

time: 117 us -> 118 us (level)
    pallas_call x1, Pallas kernels: 114 us -> 115 us  [shards(): pl.pallas_call(functools.partial(kernel, n_head, n_seq), out_shape=jax.Sh...]
where the time goes in v4:
time: 118 us
  Pallas kernels  115 us (97%)
  local copies, waits for them, and re-layouts  2.67 us (2%)
    pallas_call x1, Pallas kernels, shards(): pl.pallas_call(functools.partial(kernel, n_head, n_seq), out_shape=jax.Sh...  115 us
    unnamed x1, local copies, waits for them, and re-layouts  2.67 us

profile of v4, /device:TPU:0, one launch (start us, length us, event | category | flops | bytes accessed | tf_op | source)
XLA Modules:
  0.0 118.1 jit_solution(4328106425686646820)
XLA Ops:
  0.0 115.5 %shard_map.37 = bf16[768,1024]{1,0:T(8,128)(2,1)} custom-call(bf16[768,1024]{1,0:T(8,128)(2,1)} %tok_ref.1, bf16[3,128,1024]{2,1,0:T(8,128)(2,1)} %w_ref.1, s32[8,256]{1,0:T(8,128)} %pos_ref.1), custom_call_target="tpu_custom_call" | custom-call | tf_op jit(solution)/shard_map/pallas_call | solution.py:455
  115.5 2.7 %copy.5 = bf16[768,1024]{1,0:T(8,128)(2,1)} copy(bf16[768,1024]{1,0:T(8,128)(2,1)} %shard_map.37) | data formatting | bytes 3145728

commit v5 on v3

--- a/solution.py
+++ b/solution.py
@@ -19,6 +19,19 @@
 
 def exact(left, right):
     return jnp.dot(left, right, precision=lax.Precision.HIGHEST, preferred_element_type=F32)
+
+
+def halves(wide):
+    high = wide.astype(BF)
+    return high, (wide - high.astype(F32)).astype(BF)
+
+
+def product(left, right):
+    return (
+        jnp.dot(left[0], right[1], preferred_element_type=F32)
+        + jnp.dot(left[1], right[0], preferred_element_type=F32)
+        + jnp.dot(left[0], right[0], preferred_element_type=F32)
+    )
 
 
 def row_norms(rows):
@@ -340,20 +353,29 @@
         values_wait(zb)
     project(2, far, True)
 
+    def share_out(target):
+        return remote(
+            part.at[target], parts_in.at[chip], rs_send.at[target], rs_recv.at[chip],
+            (y, target * 2 + core),
+        )
+
     for h in range(heads):
         total = jnp.dot(kw[h], qkv[2, :, cols(h)], preferred_element_type=F32)
         for j in range(group):
-            part[h * group + j] = total[j * share : (j + 1) * share]
-    all_chips(
-        lambda i: part.at[lax.rem(chip + i, nch)], parts_in.at[chip], rs_send, rs_recv
-    )
+            target = h * group + j
+            part[target] = total[j * share : (j + 1) * share]
+            guarded(target != chip, lambda target=target: share_out(target))
+
     mine = marks_of(chip // group)
     inner = gauss(mine, mine)
     scale_cols = jnp.max(jnp.sum(jnp.abs(inner), 0, keepdims=True))
     scale_rows = jnp.max(jnp.sum(jnp.abs(inner), 1, keepdims=True))
     iterate = inner / (scale_cols * scale_rows)
+    inner_halves = halves(inner)
     for step in range(NSTEPS):
-        iterate = 2.0 * iterate - exact(exact(iterate, inner), iterate)
+        now = halves(iterate)
+        left = halves(product(now, inner_halves))
+        iterate = 2.0 * iterate - product(left, now)
     inv[...] = iterate
 
     for h in range(heads):
@@ -365,7 +387,10 @@
             return carry
 
         lax.fori_loop(0, 2 * toks // TILE, weigh_q, 0)
-    from_chips(parts_in, rs_send, rs_recv)
+    for i in range(1, nch):
+        source = lax.rem(chip + i, nch)
+        ref = parts_in.at[source]
+        remote(ref, ref, rs_send.at[source], rs_recv.at[source], chip_dev(i)).wait_recv()
     total = part[chip]
     for i in range(1, nch):
         total = total + parts_in[lax.rem(chip + i, nch)]

time: 117 us -> 116 us (level)
    pallas_call x1, Pallas kernels: 114 us -> 113 us  [shards(): pl.pallas_call(functools.partial(kernel, n_head, n_seq), out_shape=jax.Sh...]
where the time goes in v5:
time: 116 us
  Pallas kernels  113 us (97%)
  local copies, waits for them, and re-layouts  2.67 us (2%)
    pallas_call x1, Pallas kernels, shards(): pl.pallas_call(functools.partial(kernel, n_head, n_seq), out_shape=jax.Sh...  113 us
    unnamed x1, local copies, waits for them, and re-layouts  2.67 us

profile of v5, /device:TPU:0, one launch (start us, length us, event | category | flops | bytes accessed | tf_op | source)
XLA Modules:
  0.0 115.5 jit_solution(15647747654441942161)
XLA Ops:
  0.0 112.9 %shard_map.37 = bf16[768,1024]{1,0:T(8,128)(2,1)} custom-call(bf16[768,1024]{1,0:T(8,128)(2,1)} %tok_ref.1, bf16[3,128,1024]{2,1,0:T(8,128)(2,1)} %w_ref.1, s32[8,256]{1,0:T(8,128)} %pos_ref.1), custom_call_target="tpu_custom_call" | custom-call | tf_op jit(solution)/shard_map/pallas_call | solution.py:465
  112.9 2.7 %copy.5 = bf16[768,1024]{1,0:T(8,128)(2,1)} copy(bf16[768,1024]{1,0:T(8,128)(2,1)} %shard_map.37) | data formatting | bytes 3145728
